TPU v7x, 512 devices: a whole 4x8x8 slice. The times are simulated.
512 devices in a mesh: dp: 8 (over z_hi, core), ctx: 64 (over x, y, z_lo).
Axes of the slice: x: 4, y: 8, z: 8 (z_hi: 4, z_lo: 2; z = z_hi * 2 + z_lo), core: 2. Of those that a mesh axis runs over, the one named last changes fastest.
Arguments:
- query_proj: bfloat16 [8, 8192, 2560], P('dp', 'ctx'), may hold values from -12 to 12
- key_proj: bfloat16 [8, 8192, 2560], P('dp', 'ctx'), may hold values from -12 to 12
- value_proj: bfloat16 [8, 8192, 2560], P('dp', 'ctx'), may hold values from -6 to 6
- out_grad: bfloat16 [8, 8192, 2560], P('dp', 'ctx'), may hold values from -20 to 20
- out_gain: float32 [2560], replicated, may hold values from 0.1 to 1.9
Outputs:
- grad_query: bfloat16 [8, 8192, 2560], P('dp', 'ctx')
- grad_key: bfloat16 [8, 8192, 2560], P('dp', 'ctx')
- grad_value: bfloat16 [8, 8192, 2560], P('dp', 'ctx')
- grad_gain: float32 [2560], replicated
All inputs are finite; a program needn't handle non-finite values.
Results may differ from a plain program's by a relative error of at most 0.0058.
Values may be sent and summed in bfloat16 or wider, within the bound.
A program may use at most 64 MiB of HBM per device.

v0:
```python
import math

import jax
import jax.numpy as jnp
from jax import lax
from jax.sharding import PartitionSpec as P

HEADS = 20
HEAD_DIM = 128
BLOCK = 128


def body(query_proj, key_proj, value_proj, out_grad, out_gain):
    length_dev = query_proj.shape[1]
    features = query_proj.shape[2]
    blocks = length_dev // BLOCK
    score_scale = 1.0 / math.sqrt(HEAD_DIM)
    query_rows = query_proj[0].reshape(blocks, BLOCK, HEADS, HEAD_DIM)
    key_rows = key_proj[0].reshape(blocks, BLOCK, HEADS, HEAD_DIM)
    value_rows = value_proj[0].reshape(blocks, BLOCK, HEADS, HEAD_DIM)
    key_tail = key_proj[0].reshape(blocks, BLOCK, features)[:, BLOCK - 1]
    value_tail = value_proj[0].reshape(blocks, BLOCK, features)[:, BLOCK - 1]
    panel_key, panel_value = (
        lax.all_gather(key_tail, "ctx", axis=0, tiled=True),
        lax.all_gather(value_tail, "ctx", axis=0, tiled=True),
    )
    all_blocks = panel_key.shape[0]
    panel_key = panel_key.reshape(all_blocks, HEADS, HEAD_DIM)
    panel_value = panel_value.reshape(all_blocks, HEADS, HEAD_DIM)
    first_block = lax.axis_index("ctx") * blocks
    block_ids = first_block + jnp.arange(blocks)
    all_ids = jnp.arange(all_blocks)
    far_keep = all_ids[None, :] < block_ids[:, None]
    inner_ids = jnp.arange(BLOCK)
    local_keep = inner_ids[:, None] >= inner_ids[None, :]
    local_scores = (
        jnp.einsum("bqhd,bkhd->bhqk", query_rows, key_rows, preferred_element_type=jnp.float32)
        * score_scale
    )
    far_scores = (
        jnp.einsum("bqhd,shd->bhqs", query_rows, panel_key, preferred_element_type=jnp.float32)
        * score_scale
    )
    local_scores = jnp.where(local_keep[None, None], local_scores, -jnp.inf)
    far_scores = jnp.where(far_keep[:, None, None, :], far_scores, -jnp.inf)
    row_top = jnp.maximum(
        jnp.max(local_scores, axis=-1, keepdims=True), jnp.max(far_scores, axis=-1, keepdims=True)
    )
    local_exp = jnp.exp(local_scores - row_top)
    far_exp = jnp.exp(far_scores - row_top)
    row_total = jnp.sum(local_exp, axis=-1, keepdims=True) + jnp.sum(
        far_exp, axis=-1, keepdims=True
    )
    local_prob = local_exp / row_total
    far_prob = far_exp / row_total
    local_half = local_prob.astype(jnp.bfloat16)
    far_half = far_prob.astype(jnp.bfloat16)
    attended = jnp.einsum(
        "bhqk,bkhd->bqhd", local_half, value_rows, preferred_element_type=jnp.float32
    )
    attended = attended + jnp.einsum(
        "bhqs,shd->bqhd", far_half, panel_value, preferred_element_type=jnp.float32
    )
    grad_rows = out_grad[0].reshape(blocks, BLOCK, HEADS, HEAD_DIM).astype(jnp.float32)
    grad_attn = (grad_rows * out_gain.reshape(HEADS, HEAD_DIM)).astype(jnp.bfloat16)
    gain_part = jnp.sum(grad_rows * attended, axis=(0, 1)).reshape(features)
    gain_total = lax.psum(gain_part, ("dp", "ctx"))
    grad_gain = gain_total / lax.axis_size("dp")
    back_key, back_value = (
        lax.all_gather(key_tail, "ctx", axis=0, tiled=True),
        lax.all_gather(value_tail, "ctx", axis=0, tiled=True),
    )
    back_key = back_key.reshape(all_blocks, HEADS, HEAD_DIM)
    back_value = back_value.reshape(all_blocks, HEADS, HEAD_DIM)
    local_dprob = jnp.einsum(
        "bqhd,bkhd->bhqk", grad_attn, value_rows, preferred_element_type=jnp.float32
    )
    far_dprob = jnp.einsum(
        "bqhd,shd->bhqs", grad_attn, back_value, preferred_element_type=jnp.float32
    )
    row_dot = jnp.sum(local_prob * local_dprob, axis=-1, keepdims=True) + jnp.sum(
        far_prob * far_dprob, axis=-1, keepdims=True
    )
    local_dscore = (local_prob * (local_dprob - row_dot)).astype(jnp.bfloat16)
    far_dscore = (far_prob * (far_dprob - row_dot)).astype(jnp.bfloat16)
    far_gkey = (
        jnp.einsum("bhqs,bqhd->shd", far_dscore, query_rows, preferred_element_type=jnp.float32)
        * score_scale
    )
    far_gvalue = jnp.einsum(
        "bhqs,bqhd->shd", far_half, grad_attn, preferred_element_type=jnp.float32
    )
    far_gkey = far_gkey.reshape(all_blocks, features)
    far_gvalue = far_gvalue.reshape(all_blocks, features)
    grad_query = jnp.einsum(
        "bhqk,bkhd->bqhd", local_dscore, key_rows, preferred_element_type=jnp.float32
    )
    grad_query = (
        grad_query
        + jnp.einsum("bhqs,shd->bqhd", far_dscore, back_key, preferred_element_type=jnp.float32)
    ) * score_scale
    local_gkey = (
        jnp.einsum("bhqk,bqhd->bkhd", local_dscore, query_rows, preferred_element_type=jnp.float32)
        * score_scale
    )
    local_gvalue = jnp.einsum(
        "bhqk,bqhd->bkhd", local_half, grad_attn, preferred_element_type=jnp.float32
    )
    mine_key, mine_value = (
        lax.psum_scatter(far_gkey, "ctx", scatter_dimension=0, tiled=True),
        lax.psum_scatter(far_gvalue, "ctx", scatter_dimension=0, tiled=True),
    )
    grad_key = local_gkey.reshape(blocks, BLOCK, features).at[:, BLOCK - 1].add(mine_key)
    grad_value = local_gvalue.reshape(blocks, BLOCK, features).at[:, BLOCK - 1].add(mine_value)
    grad_query = grad_query.reshape(1, length_dev, features).astype(jnp.bfloat16)
    grad_key = grad_key.astype(jnp.bfloat16)
    grad_value = grad_value.astype(jnp.bfloat16)
    return (grad_query, grad_key, grad_value, grad_gain)


def solution(mesh):
    in_specs = (
        P("dp", "ctx", None),
        P("dp", "ctx", None),
        P("dp", "ctx", None),
        P("dp", "ctx", None),
        P(),
    )
    out_specs = (P("dp", "ctx", None), P("dp", "ctx", None), P("dp", "ctx", None), P())
    return jax.shard_map(body, mesh=mesh, in_specs=in_specs, out_specs=out_specs, check_vma=False)
```

profile of v0, /device:TPU:8, one launch (start us, length us, event | category | flops | bytes accessed | tf_op | source)
XLA Modules:
  0.0 955.9 jit_solution(14411527670212340184)
XLA Ops:
  7.3 1.5 copy.58
  8.8 0.8 slice.50
  9.6 1.1 copy.64
  11.1 156.6 %all-gather = bf16[64,1,2560]{2,1,0:T(2,128)(2,1)S(1)} all-gather(bf16[1,1,2560]{2,1,0:T(2,128)(2,1)S(1)} %slice.50), channel_id=2, replica_groups=mesh['dp'=8,'ctx'=64] {'ctx'}, dimensions={0}, use_global_device_ids=true | all-gather | bytes 332800 | tf_op jit(solution)/shard_map/all_gather | solution.py:24
  167.6 1.9 reduce.13
  170.6 0.8 copy-done.2
  171.9 1.1 copy.63
  173.0 1.2 convert_element_type.80
  174.2 163.6 %all-gather.1 = bf16[64,1,2560]{2,1,0:T(2,128)(2,1)} all-gather(bf16[1,1,2560]{2,1,0:T(2,128)(2,1)S(1)} %slice.51), channel_id=3, replica_groups=mesh['dp'=8,'ctx'=64] {'ctx'}, dimensions={0}, use_global_device_ids=true | all-gather | bytes 332800 | tf_op jit(solution)/shard_map/all_gather | solution.py:71
  337.8 3.6 reduce.14
  341.8 0.7 copy-done.3
  342.5 0.5 convolution_bitcast_fusion.5
  343.0 0.9 copy.125
  344.5 0.7 copy-done.18
  345.2 1.5 multiply_reduce_fusion
  346.9 0.5 fusion.7
  347.5 0.9 copy.126
  348.4 2.9 fusion.23
  351.7 1.7 convolution_multiply_fusion
  353.3 1.5 copy.84
  354.8 2.8 copy.80
  357.6 2.9 copy.75
  360.9 0.6 copy-done.10
  362.0 1.1 copy.85
  363.1 1.3 dynamic-slice.16
  364.4 0.6 convolution_bitcast_fusion.1
  366.4 103.3 %psum.7 = f32[2560]{0:T(1024)S(1)} all-reduce(f32[2560]{0:T(1024)S(1)} %bitcast.158), channel_id=1, replica_groups=mesh['dp'=8,'ctx'=64] {'dp','ctx'}, use_global_device_ids=true, to_apply=%region_9.10 | all-reduce | flops 2560 | bytes 20480 | tf_op jit(solution)/shard_map/psum | solution.py:67
  469.7 0.6 broadcast_multiply_fusion
  470.3 474.9 %all-reduce.5.cloned.1.call-done = (f32[64,2560]{1,0:T(8,128)}, f32[64,2560]{1,0:T(8,128)}) async-done(((f32[64,2560]{1,0:T(8,128)}, f32[64,2560]{1,0:T(8,128)}), (f32[64,2560]{1,0:T(8,128)}, f32[64,2560]{1,0:T(8,128)})) %all-reduce.5.cloned.1.call-update) | async-done | bytes 1310736
  945.2 1.6 slice_add_fusion
  947.0 0.9 convert_element_type.77
  948.2 0.9 convert_element_type.74
  (66 shorter events, 6.0 us)
Async XLA Ops:
  7.2 2.4 copy-start.15
  7.2 938.0 %all-reduce.5.cloned.1.call-start = ((), (), s32[]{:S(2)}) async-start(), calls=%async_computation | async-start | bytes 2621440
  7.2 3.5 copy-start.16
  8.8 160.8 %copy-start.5 = (bf16[1,128,2560]{1,2,0:T(8,128)(2,1)}, bf16[1,128,2560]{1,2,0:T(8,128)(2,1)S(1)}, u32[]{:S(2)}) copy-start(bf16[1,128,2560]{1,2,0:T(8,128)(2,1)S(1)} %copy.58) | copy-start | bytes 1966084
  169.6 0.7 copy-start.9
  170.6 0.8 copy-start.2
  170.6 1.3 copy-start.17
  174.2 167.2 %copy-start.23 = (f32[2560]{0:T(1024)S(1)}, f32[2560]{0:T(1024)}, u32[]{:S(2)}) copy-start(f32[2560]{0:T(1024)} %param.13) | copy-start | bytes 30724
  341.4 1.1 copy-start.3
  342.5 2.0 copy-start.20
  343.0 1.1 copy-start.21
  344.1 1.1 copy-start.18
  346.9 1.5 copy-start.11
  348.4 2.9 copy-start.13
  351.7 1.7 copy-start
  357.6 2.9 copy-start.1
  357.6 2.9 copy-start.6
  360.5 1.0 copy-start.10
  360.5 1.1 copy-start.12
  362.0 2.4 copy-start.19
  364.4 1.1 copy-start.4
  364.4 1.5 copy-start.14
  364.4 1.6 copy-start.22
  365.9 579.2 %copy-start.7 = (f32[1,128,2560]{2,1,0:T(8,128)S(1)}, f32[1,128,2560]{2,1,0:T(8,128)}, u32[]{:S(2)}) copy-start(f32[1,128,2560]{2,1,0:T(8,128)} %copy.75) | copy-start | bytes 3932164
  365.9 579.2 %copy-start.8 = (f32[1,128,2560]{2,1,0:T(8,128)S(1)}, f32[1,128,2560]{2,1,0:T(8,128)}, u32[]{:S(2)}) copy-start(f32[1,128,2560]{2,1,0:T(8,128)} %copy.80) | copy-start | bytes 3932164
Sparse Core Ops, SparseCore 0:
  348.5 596.5 all-reduce.4
where the time goes:
time: 957 us; the launch traced here: 956 us
  waiting for transfers between devices  475 us (50%)
  blocking collectives  423 us (44%)
  local copies, waits for them, and re-layouts  21.3 us (2%)
  between operations  14.3 us (1%)
  other arithmetic  12.1 us (1%)
  matrix products  9.88 us (1%)
    unnamed x2, waiting for transfers between devices  475 us
    all_gather x1, blocking collectives, body(): lax.all_gather(value_tail, 'ctx', axis=0, tiled=True)  164 us
    all_gather x1, blocking collectives, body(): lax.all_gather(key_tail, 'ctx', axis=0, tiled=True)  157 us
    psum x1, blocking collectives, body(): gain_total = lax.psum(gain_part, ('dp', 'ctx'))  103 us
  transfers between devices with their start and end apart: 1, of which 1 were waited for; matrix products, arithmetic and copies ran while one was open for 2% of the time, Pallas kernels for 0%

commit v1 on v0

v1 whole, which is shorter than its diff:
```python
import functools
import math

import jax
import jax.numpy as jnp
from jax import lax
from jax.experimental import pallas as pl
from jax.experimental.pallas import tpu as pltpu
from jax.sharding import PartitionSpec as P

DIM = 128
BLOCK = 128
NX, NY, NZ = 4, 8, 2
GROUPS = 2
MESH = pl.DeviceIdType.MESH
F32 = jnp.float32
BF16 = jnp.bfloat16


def dot(a, b, dims):
    return lax.dot_general(a, b, (dims, ((), ())), preferred_element_type=F32)


def kernel(
    heads, ndp,
    q_hbm, k_hbm, v_hbm, g_hbm, gain_ref,
    gq_hbm, gk_hbm, gv_hbm, gg_ref,
    qv, kc, vc, gv, gqo, gko, gvo, lastk, lastv, st, dpt,
    tails, send, rbuf, acc, pairs, asend, arecv, gpart, gb1, gb2, gb3,
    insem, outsem, a_s, a_r, b_s, b_r, c_s, c_r, d_s, d_r, g_s, g_r,
):
    features = heads * DIM
    plane = NY * NZ
    blocks = NX * plane
    scale = 1.0 / math.sqrt(DIM)
    escale = scale * math.log2(math.e)
    dp = lax.axis_index("dp")
    me = lax.axis_index("ctx")
    ip = lax.rem(me, plane)
    ix = lax.div(me, plane)
    iy = lax.div(ip, NZ)
    iz = lax.rem(ip, NZ)
    row0 = pl.multiple_of(BLOCK + ix * plane, plane)

    def ctx_of(x, y, z):
        return x * plane + y * NZ + z

    first = BLOCK - 16
    loads = []
    for n, (src, dst) in enumerate(((k_hbm, kc), (v_hbm, vc))):
        cp = pltpu.make_async_copy(src.at[pl.ds(first, 16)], dst.at[pl.ds(first, 16)], insem.at[n])
        cp.start()
        loads.append(cp)
    for n, (src, dst) in enumerate(((k_hbm, kc), (v_hbm, vc))):
        cp = pltpu.make_async_copy(src.at[pl.ds(0, first)], dst.at[pl.ds(0, first)], insem.at[2 + n])
        cp.start()
        loads.append(cp)
    for n, (src, dst) in enumerate(((q_hbm, qv), (g_hbm, gv))):
        cp = pltpu.make_async_copy(src, dst, insem.at[4 + n])
        cp.start()
        loads.append(cp)

    kc[BLOCK:] = jnp.zeros((blocks, features), BF16)
    vc[BLOCK:] = jnp.zeros((blocks, features), BF16)

    barrier = pltpu.get_barrier_semaphore()
    count = 0

    def greet(device):
        pl.semaphore_signal(barrier, inc=1, device_id=device, device_id_type=MESH)

    for j in range(1, plane):
        greet({"ctx": ix * plane + lax.rem(ip + j, plane)})
        count += 1
    for j in range(1, NX):
        for dz in range(NZ):
            greet({"ctx": ctx_of(lax.rem(ix + j, NX), iy, lax.rem(iz + dz, NZ))})
            count += 1
    for j in range(1, ndp):
        greet({"dp": lax.rem(dp + j, ndp)})
        count += 1

    loads[0].wait()
    loads[1].wait()
    ktail = kc[pl.ds(first, 16)].astype(F32)[15:16]
    vtail = vc[pl.ds(first, 16)].astype(F32)[15:16]
    tails[ip] = jnp.concatenate([ktail, vtail], axis=0).astype(BF16)

    pl.semaphore_wait(barrier, count)

    def a_copy(j):
        p = lax.rem(ip + j, plane)
        return pltpu.make_async_remote_copy(
            src_ref=tails.at[ip], dst_ref=tails.at[ip], send_sem=a_s.at[j], recv_sem=a_r.at[ip],
            device_id={"ctx": ix * plane + p}, device_id_type=MESH)

    def a_wait(j):
        p = lax.rem(ip + j, plane)
        pltpu.make_async_remote_copy(
            src_ref=tails.at[p], dst_ref=tails.at[p], send_sem=a_s.at[j], recv_sem=a_r.at[p],
            device_id={"ctx": ix * plane + p}, device_id_type=MESH).wait_recv()

    for j in range(1, plane):
        a_copy(j).start()

    for n in range(2, 6):
        loads[n].wait()

    key_id = lax.broadcasted_iota(jnp.int32, (BLOCK, BLOCK), 0)
    query_id = lax.broadcasted_iota(jnp.int32, (BLOCK, BLOCK), 1)
    far_id = lax.broadcasted_iota(jnp.int32, (blocks, BLOCK), 0)
    neg = -jnp.inf

    def cols(h, base=0):
        return pl.ds(pl.multiple_of(h * DIM + base, DIM), DIM)

    def local_part(h, _):
        c = cols(h)
        g = gv[:, c]
        ga = (g.astype(F32) * gain_ref[:, c]).astype(BF16)
        s = dot(kc[pl.ds(0, BLOCK), c], qv[:, c], ((1,), (1,)))
        st[h] = jnp.where(key_id <= query_id, s, neg)
        dpt[h] = dot(vc[pl.ds(0, BLOCK), c], ga, ((1,), (1,)))
        return 0

    half = heads // 2
    lax.fori_loop(0, half, local_part, 0)

    for j in range(1, plane):
        a_wait(j)
    for i in range(plane):
        pairs[pl.ds(2 * i, 2)] = tails[i].astype(F32)
    to_id = lax.broadcasted_iota(jnp.int32, (2 * plane, 2 * plane), 0)
    from_id = lax.broadcasted_iota(jnp.int32, (2 * plane, 2 * plane), 1)
    apart = jnp.where(from_id == 2 * lax.rem(to_id, plane) + lax.div(to_id, plane), 1.0, 0.0).astype(BF16)
    sorted_rows = dot(apart, pairs[...].astype(BF16), ((1,), (0,)))
    kc[pl.ds(row0, plane)] = sorted_rows[:plane].astype(BF16)
    vc[pl.ds(row0, plane)] = sorted_rows[plane:].astype(BF16)

    def b_copy(d, n, start):
        buf = (kc, vc)[n]
        row = start
        return pltpu.make_async_remote_copy(
            src_ref=buf.at[pl.ds(row, plane)], dst_ref=buf.at[pl.ds(row, plane)],
            send_sem=b_s.at[d, n], recv_sem=b_r.at[d, n],
            device_id={"ctx": lax.rem(ix + d, NX) * plane + ip}, device_id_type=MESH)

    for d in range(1, NX):
        @pl.when(ix + d < NX)
        def _():
            for n in range(2):
                b_copy(d, n, row0).start()

    lax.fori_loop(half, heads, local_part, 0)

    for d in range(1, NX):
        @pl.when(ix - d >= 0)
        def _():
            for n in range(2):
                b_copy(d, n, pl.multiple_of(BLOCK + (ix - d) * plane, plane)).wait_recv()

    far_keep = far_id < me

    def full_part(h, _):
        c = cols(h)
        q = qv[:, c]
        g = gv[:, c]
        ga = (g.astype(F32) * gain_ref[:, c]).astype(BF16)
        kh = kc[:, c]
        vh = vc[:, c]
        s_far = jnp.where(far_keep, dot(kc[pl.ds(BLOCK, blocks), c], q, ((1,), (1,))), neg)
        dp_far = dot(vc[pl.ds(BLOCK, blocks), c], ga, ((1,), (1,)))
        s = jnp.concatenate([st[h], s_far], axis=0)
        dprob = jnp.concatenate([dpt[h], dp_far], axis=0)
        top = jnp.max(s, axis=0, keepdims=True)
        e = jnp.exp2((s - top) * escale)
        prob = e * (1.0 / jnp.sum(e, axis=0, keepdims=True))
        row_dot = jnp.sum(prob * dprob, axis=0, keepdims=True)
        ds = (prob * (dprob - row_dot)).astype(BF16)
        ph = prob.astype(BF16)
        both = dot(ph, jnp.concatenate([g, ga], axis=1), ((1,), (0,)))
        gpart[:, c] = jnp.sum(vh.astype(F32) * both[:, :DIM], axis=0, keepdims=True)
        gval = both[:, DIM:]
        gkey = dot(ds, q, ((1,), (0,))) * scale
        gqo[:, c] = (dot(ds, kh, ((0,), (0,))) * scale).astype(BF16)
        gko[:, c] = gkey[:BLOCK].astype(BF16)
        gvo[:, c] = gval[:BLOCK].astype(BF16)
        lastk[:, c] = gkey[first:BLOCK]
        lastv[:, c] = gval[first:BLOCK]
        send[:, c] = gkey[BLOCK:].astype(BF16)
        send[:, cols(h, features)] = gval[BLOCK:].astype(BF16)
        return 0

    width = features // GROUPS

    def c_copy(d, grp, n):
        lo = pl.multiple_of(lax.rem(ix - d + NX, NX) * plane, plane)
        cc = pl.ds(n * features + grp * width, width)
        return pltpu.make_async_remote_copy(
            src_ref=send.at[pl.ds(lo, plane), cc], dst_ref=rbuf.at[d - 1, :, cc],
            send_sem=c_s.at[d - 1, grp, n], recv_sem=c_r.at[d - 1, grp, n],
            device_id={"ctx": lax.rem(ix - d + NX, NX) * plane + ip}, device_id_type=MESH)

    per = heads // GROUPS
    for grp in range(GROUPS):
        lax.fori_loop(grp * per, (grp + 1) * per, full_part, 0)
        for d in range(1, NX):
            @pl.when(ix - d >= 0)
            def _():
                for n in range(2):
                    c_copy(d, grp, n).start()

    gain_groups = (
        (NY, iy, lambda o: {"ctx": ctx_of(ix, o, iz)}),
        (NX * NZ, ix * NZ + iz, lambda o: {"ctx": ctx_of(lax.div(o, NZ), iy, lax.rem(o, NZ))}),
        (ndp, dp, lambda o: {"dp": o}),
    )

    def gain_copy(stage, j, slot):
        size, mine, where = gain_groups[stage]
        buf = (gb1, gb2, gb3)[stage]
        other = lax.rem(mine + j, size)
        s = mine if slot is None else other
        return pltpu.make_async_remote_copy(
            src_ref=buf.at[s], dst_ref=buf.at[s], send_sem=g_s.at[stage, j], recv_sem=g_r.at[stage, s],
            device_id=where(other), device_id_type=MESH)

    def gain_start(stage, value):
        size, mine, _ = gain_groups[stage]
        (gb1, gb2, gb3)[stage][mine] = value
        for j in range(1, size):
            gain_copy(stage, j, None).start()

    def gain_end(stage):
        size, _, _ = gain_groups[stage]
        for j in range(1, size):
            gain_copy(stage, j, 1).wait_recv()
        buf = (gb1, gb2, gb3)[stage]
        total = buf[0]
        for i in range(1, size):
            total = total + buf[i]
        return total

    gain_start(0, gpart[...])

    pltpu.make_async_copy(gqo, gq_hbm, outsem.at[0]).start()
    for n, (src, dst) in enumerate(((gko, gk_hbm), (gvo, gv_hbm))):
        pltpu.make_async_copy(src.at[pl.ds(0, first)], dst.at[pl.ds(0, first)], outsem.at[1 + n]).start()

    acc[...] = send[pl.ds(pl.multiple_of(ix * plane, plane), plane)].astype(F32)
    gain_start(1, gain_end(0))
    for d in range(1, NX):
        @pl.when(ix + d < NX)
        def _():
            for grp in range(GROUPS):
                for n in range(2):
                    c_copy(d, grp, n).wait_recv()
            acc[...] += rbuf[d - 1].astype(F32)

    both_rows = jnp.concatenate([acc[:, :features], acc[:, features:]], axis=0).astype(BF16)
    pairs[...] = dot(apart, both_rows, ((0,), (0,)))
    for i in range(plane):
        asend[i] = pairs[pl.ds(2 * i, 2)].astype(BF16)

    def d_copy(j, recv):
        p = lax.rem(ip + j, plane)
        return pltpu.make_async_remote_copy(
            src_ref=asend.at[p], dst_ref=arecv.at[p if recv else ip],
            send_sem=d_s.at[j], recv_sem=d_r.at[p if recv else ip],
            device_id={"ctx": ix * plane + p}, device_id_type=MESH)

    for j in range(1, plane):
        d_copy(j, False).start()
    arecv[ip] = asend[ip]
    gain_start(2, gain_end(1))
    for j in range(1, plane):
        d_copy(j, True).wait_recv()
    total = arecv[0].astype(F32)
    for i in range(1, plane):
        total = total + arecv[i].astype(F32)
    last = lax.broadcasted_iota(jnp.int32, (16, features), 0) == 15
    gko[pl.ds(first, 16)] = (lastk[...] + jnp.where(last, total[0:1], 0.0)).astype(BF16)
    gvo[pl.ds(first, 16)] = (lastv[...] + jnp.where(last, total[1:2], 0.0)).astype(BF16)
    for n, (src, dst) in enumerate(((gko, gk_hbm), (gvo, gv_hbm))):
        pltpu.make_async_copy(src.at[pl.ds(first, 16)], dst.at[pl.ds(first, 16)], outsem.at[3 + n]).start()

    gg_ref[...] = gain_end(2) * (1.0 / ndp)

    pltpu.make_async_copy(gqo, gq_hbm, outsem.at[0]).wait()
    for n, (src, dst) in enumerate(((gko, gk_hbm), (gvo, gv_hbm))):
        pltpu.make_async_copy(src.at[pl.ds(0, first)], dst.at[pl.ds(0, first)], outsem.at[1 + n]).wait()
        pltpu.make_async_copy(src.at[pl.ds(first, 16)], dst.at[pl.ds(first, 16)], outsem.at[3 + n]).wait()
    for j in range(1, plane):
        a_copy(j).wait_send()
        d_copy(j, False).wait_send()
    for d in range(1, NX):
        @pl.when(ix + d < NX)
        def _():
            for n in range(2):
                b_copy(d, n, row0).wait_send()

        @pl.when(ix - d >= 0)
        def _():
            for grp in range(GROUPS):
                for n in range(2):
                    c_copy(d, grp, n).wait_send()
    for stage in range(3):
        for j in range(1, gain_groups[stage][0]):
            gain_copy(stage, j, None).wait_send()


def body(ndp, query_proj, key_proj, value_proj, out_grad, out_gain):
    features = query_proj.shape[2]
    heads = features // DIM
    plane = NY * NZ
    blocks = NX * plane
    flat = lambda a: a.reshape(BLOCK, features)
    any_spec = pl.BlockSpec(memory_space=pl.ANY)
    vmem_spec = pl.BlockSpec(memory_space=pltpu.VMEM)
    dma = pltpu.SemaphoreType.DMA
    rows = jax.ShapeDtypeStruct((BLOCK, features), BF16)
    outs = pl.pallas_call(
        functools.partial(kernel, heads, ndp),
        out_shape=(rows, rows, rows, jax.ShapeDtypeStruct((1, features), F32)),
        in_specs=[any_spec] * 4 + [vmem_spec],
        out_specs=(any_spec, any_spec, any_spec, vmem_spec),
        scratch_shapes=[
            pltpu.VMEM((BLOCK, features), BF16),
            pltpu.VMEM((BLOCK + blocks, features), BF16),
            pltpu.VMEM((BLOCK + blocks, features), BF16),
            pltpu.VMEM((BLOCK, features), BF16),
            pltpu.VMEM((BLOCK, features), BF16),
            pltpu.VMEM((BLOCK, features), BF16),
            pltpu.VMEM((BLOCK, features), BF16),
            pltpu.VMEM((16, features), F32),
            pltpu.VMEM((16, features), F32),
            pltpu.VMEM((heads, BLOCK, BLOCK), F32),
            pltpu.VMEM((heads, BLOCK, BLOCK), F32),
            pltpu.VMEM((plane, 2, features), BF16),
            pltpu.VMEM((blocks, 2 * features), BF16),
            pltpu.VMEM((NX - 1, plane, 2 * features), BF16),
            pltpu.VMEM((plane, 2 * features), F32),
            pltpu.VMEM((2 * plane, features), F32),
            pltpu.VMEM((plane, 2, features), BF16),
            pltpu.VMEM((plane, 2, features), BF16),
            pltpu.VMEM((1, features), F32),
            pltpu.VMEM((NY, 1, features), F32),
            pltpu.VMEM((NX * NZ, 1, features), F32),
            pltpu.VMEM((ndp, 1, features), F32),
            dma((6,)),
            dma((5,)),
            dma((plane,)),
            dma((plane,)),
            dma((NX, 2)),
            dma((NX, 2)),
            dma((NX - 1, GROUPS, 2)),
            dma((NX - 1, GROUPS, 2)),
            dma((plane,)),
            dma((plane,)),
            dma((3, max(NY, NX * NZ, ndp))),
            dma((3, max(NY, NX * NZ, ndp))),
        ],
        compiler_params=pltpu.CompilerParams(
            collective_id=0, has_side_effects=True, vmem_limit_bytes=56 * 1024 * 1024
        ),
    )(flat(query_proj), flat(key_proj), flat(value_proj), flat(out_grad), out_gain.reshape(1, features))
    shape = (1, BLOCK, features)
    return (outs[0].reshape(shape), outs[1].reshape(shape), outs[2].reshape(shape), outs[3].reshape(features))


def solution(mesh):
    spec = P("dp", "ctx", None)
    return jax.shard_map(
        functools.partial(body, mesh.shape["dp"]),
        mesh=mesh,
        in_specs=(spec, spec, spec, spec, P()),
        out_specs=(spec, spec, spec, P()),
        check_vma=False,
    )
```

time: 957 us -> 65.9 us (0.07)
  the two profiles are of different devices: /device:TPU:8 before, /device:TPU:1 now
where the time goes in v1:
time: 65.9 us; the launch traced here: 65.5 us
  Pallas kernels  58 us (88%)
  local copies, waits for them, and re-layouts  6.2 us (9%)
    pallas_call x1, Pallas kernels, body(): pl.pallas_call(functools.partial(kernel, heads, ndp), out_shape=(rows, ro...  58 us
    unnamed x9, local copies, waits for them, and re-layouts  4.89 us

profile of v1, /device:TPU:1, one launch (start us, length us, event | category | flops | bytes accessed | tf_op | source)
XLA Modules:
  0.0 65.5 jit_solution(3094913258143786784)
XLA Ops:
  0.6 1.3 %reshape.39.gain_ref = f32[1,2560]{1,0:T(1,128)} reshape(f32[2560]{0:T(1024)} %param.9) | data formatting | bytes 20480 | tf_op jit(solution)/shard_map/reshape | solution.py:366
  1.9 58.0 %shard_map.84 = (bf16[128,2560]{1,0:T(8,128)(2,1)}, bf16[128,2560]{1,0:T(8,128)(2,1)}, bf16[128,2560]{1,0:T(8,128)(2,1)}, f32[1,2560]{1,0:T(1,128)}) custom-call(bf16[128,2560]{1,0:T(8,128)(2,1)} %bitcast.10, bf16[128,2560]{1,0:T(8,128)(2,1)} %bitcast.11, bf16[128,2560]{1,0:T(8,128)(2,1)} %bitcast.12, bf16[128,2560]{1,0:T(8,128)(2,1)} %bitcast.13, ...), custom_call_target="tpu_custom_call" | custom-call | tf_op jit(solution)/shard_map/pallas_call | solution.py:322
  60.0 0.0 copy-start.2
  60.0 0.7 %copy-done.2 = f32[1,2560]{1,0:T(1,128)S(1)} copy-done((f32[1,2560]{1,0:T(1,128)S(1)}, f32[1,2560]{1,0:T(1,128)}, u32[]{:S(2)}) %copy-start.2) | copy-done | bytes 10264
  60.7 0.6 reduce
  61.3 0.0 copy-start.1
  61.3 2.0 %copy.12 = bf16[1,128,2560]{2,1,0:T(8,128)(2,1)} copy(bf16[1,128,2560]{2,1,0:T(8,128)(2,1)} %bitcast.9) | data formatting | bytes 1310720
  63.3 0.0 copy-done.1
  63.3 0.0 copy-start
  63.3 0.8 %copy.13 = bf16[1,128,2560]{2,1,0:T(8,128)(2,1)} copy(bf16[1,128,2560]{2,1,0:T(8,128)(2,1)S(1)} %bitcast.8) | data formatting | bytes 1310720
  64.2 0.5 copy-done
  64.7 0.8 %copy.14 = bf16[1,128,2560]{2,1,0:T(8,128)(2,1)} copy(bf16[1,128,2560]{2,1,0:T(8,128)(2,1)S(1)} %bitcast.7) | data formatting | bytes 1310720
Async XLA Ops:
  60.0 0.7 %copy-start.2 = (f32[1,2560]{1,0:T(1,128)S(1)}, f32[1,2560]{1,0:T(1,128)}, u32[]{:S(2)}) copy-start(f32[1,2560]{1,0:T(1,128)} %get-tuple-element.11) | copy-start | bytes 30724
  61.3 2.0 %copy-start.1 = (bf16[128,2560]{1,0:T(8,128)(2,1)S(1)}, bf16[128,2560]{1,0:T(8,128)(2,1)}, u32[]{:S(2)}) copy-start(bf16[128,2560]{1,0:T(8,128)(2,1)} %get-tuple-element.9) | copy-start | bytes 1966084
  63.3 1.3 %copy-start = (bf16[128,2560]{1,0:T(8,128)(2,1)S(1)}, bf16[128,2560]{1,0:T(8,128)(2,1)}, u32[]{:S(2)}) copy-start(bf16[128,2560]{1,0:T(8,128)(2,1)} %get-tuple-element.10) | copy-start | bytes 1966084

commit v2 on v0

v2 whole, which is shorter than its diff:
```python
import functools
import math

import jax
import jax.numpy as jnp
from jax import lax
from jax.experimental import pallas as pl
from jax.experimental.pallas import tpu as pltpu
from jax.sharding import PartitionSpec as P

DIM = 128
BLOCK = 128
NX, NY, NZ = 4, 8, 2
CHUNKS = 4
MESH = pl.DeviceIdType.MESH
F32 = jnp.float32
BF16 = jnp.bfloat16


def dot(a, b, dims):
    return lax.dot_general(a, b, (dims, ((), ())), preferred_element_type=F32)


def kernel(
    heads, ndp,
    q_hbm, k_hbm, v_hbm, g_hbm, gain_hbm,
    gqo, gko, gvo, gg_ref,
    qv, kc, vc, gv, gav, gain_ref, lastk, lastv, st, dpt,
    gvf, tails, panel, send, rbuf, acc, pairs, dsend, drecv, gpart, gb1, gb2, gb3,
    insem, a_s, a_r, b_s, b_r, c_s, c_r, d_s, d_r, g_s, g_r,
):
    features = heads * DIM
    nb = NX * NZ
    blocks = NX * NY * NZ
    per = heads // CHUNKS
    width = per * DIM
    scale = 1.0 / math.sqrt(DIM)
    escale = scale * math.log2(math.e)
    dp = lax.axis_index("dp")
    me = lax.axis_index("ctx")
    ix = lax.div(me, NY * NZ)
    iy = lax.rem(lax.div(me, NZ), NY)
    iz = lax.rem(me, NZ)
    ib = ix * NZ + iz

    def y_peer(o):
        return {"ctx": (ix * NY + o) * NZ + iz}

    def b_peer(o):
        return {"ctx": (lax.div(o, NZ) * NY + iy) * NZ + lax.rem(o, NZ)}

    def dp_peer(o):
        return {"dp": o}

    first = BLOCK - 16
    loads = []

    def load(n, src, dst):
        cp = pltpu.make_async_copy(src, dst, insem.at[n])
        cp.start()
        loads.append(cp)

    load(0, k_hbm.at[pl.ds(first, 16)], kc.at[pl.ds(first, 16)])
    load(1, v_hbm.at[pl.ds(first, 16)], vc.at[pl.ds(first, 16)])
    load(2, k_hbm.at[pl.ds(0, first)], kc.at[pl.ds(0, first)])
    load(3, q_hbm, qv)
    load(4, v_hbm.at[pl.ds(0, first)], vc.at[pl.ds(0, first)])
    load(5, g_hbm, gv)
    load(6, gain_hbm, gain_ref)

    panel[...] = jnp.zeros_like(panel)

    barrier = pltpu.get_barrier_semaphore()

    def greet(device):
        pl.semaphore_signal(barrier, inc=1, device_id=device, device_id_type=MESH)

    for j in range(1, NY):
        greet(y_peer(lax.rem(iy + j, NY)))
    for j in range(1, nb):
        greet(b_peer(lax.rem(ib + j, nb)))
    for j in range(1, ndp):
        greet(dp_peer(lax.rem(dp + j, ndp)))

    loads[0].wait()
    loads[1].wait()
    ktail = kc[pl.ds(first, 16)].astype(F32)[15:16]
    vtail = vc[pl.ds(first, 16)].astype(F32)[15:16]
    tails[iy] = jnp.concatenate([ktail, vtail], axis=0).astype(BF16)

    pl.semaphore_wait(barrier, NY + nb + ndp - 3)

    def a_copy(j, recv):
        p = lax.rem(iy + j, NY)
        s = p if recv else iy
        return pltpu.make_async_remote_copy(
            src_ref=tails.at[s], dst_ref=tails.at[s], send_sem=a_s.at[j], recv_sem=a_r.at[s],
            device_id=y_peer(p), device_id_type=MESH)

    for j in range(1, NY):
        a_copy(j, False).start()

    key_id = lax.broadcasted_iota(jnp.int32, (BLOCK, BLOCK), 0)
    query_id = lax.broadcasted_iota(jnp.int32, (BLOCK, BLOCK), 1)
    neg = -jnp.inf

    def cols(h):
        return pl.ds(pl.multiple_of(h * DIM, DIM), DIM)

    def local_scores(h, _):
        c = cols(h)
        s = dot(kc[pl.ds(0, BLOCK), c], qv[:, c], ((1,), (1,)))
        st[h, pl.ds(0, BLOCK)] = jnp.where(key_id <= query_id, s, neg)
        return 0

    def local_dprob(h, _):
        c = cols(h)
        ga = (gv[:, c].astype(F32) * gain_ref[pl.ds(h, 1), :]).astype(BF16)
        gav[:, c] = ga
        dpt[h] = dot(vc[pl.ds(0, BLOCK), c], ga, ((1,), (1,)))
        return 0

    loads[2].wait()
    loads[3].wait()
    lax.fori_loop(0, heads, local_scores, 0, unroll=per)
    loads[4].wait()
    loads[5].wait()
    loads[6].wait()
    lax.fori_loop(0, heads, local_dprob, 0, unroll=per)

    for j in range(1, NY):
        a_copy(j, True).wait_recv()
    for i in range(NY):
        pairs[pl.ds(2 * i, 2)] = tails[i].astype(F32)
    to_id = lax.broadcasted_iota(jnp.int32, (2 * NY, 2 * NY), 0)
    from_id = lax.broadcasted_iota(jnp.int32, (2 * NY, 2 * NY), 1)
    apart = jnp.where(from_id == 2 * lax.rem(to_id, NY) + lax.div(to_id, NY), 1.0, 0.0).astype(BF16)
    panel[ib] = dot(apart, pairs[...].astype(BF16), ((1,), (0,))).astype(BF16)

    def chunk(c):
        return pl.ds(c * width, width)

    def b_copy(c, j, recv):
        p = lax.rem(ib + j, nb)
        s = p if recv else ib
        return pltpu.make_async_remote_copy(
            src_ref=panel.at[s, :, chunk(c)], dst_ref=panel.at[s, :, chunk(c)],
            send_sem=b_s.at[c, j], recv_sem=b_r.at[c, s],
            device_id=b_peer(p), device_id_type=MESH)

    def later(j):
        return lax.div(lax.rem(ib + j, nb), NZ) >= ix

    def earlier(j):
        return lax.div(lax.rem(ib + j, nb), NZ) <= ix

    for c in range(CHUNKS):
        for j in range(1, nb):
            @pl.when(later(j))
            def _():
                b_copy(c, j, False).start()

    row = lax.broadcasted_iota(jnp.int32, (blocks, BLOCK), 0)
    far_id = (lax.div(row, NY * NZ) * NY + lax.rem(row, NY)) * NZ + lax.rem(lax.div(row, NY), NZ)
    far_keep = far_id < me
    far = pl.ds(BLOCK, blocks)

    def forward(h, _):
        c = cols(h)
        s_far = jnp.where(far_keep, dot(kc[far, c], qv[:, c], ((1,), (1,))), neg)
        s = jnp.concatenate([st[h, pl.ds(0, BLOCK)], s_far], axis=0)
        top = jnp.max(s, axis=0, keepdims=True)
        e = jnp.exp2((s - top) * escale)
        prob = e * (1.0 / jnp.sum(e, axis=0, keepdims=True))
        st[h] = prob
        both = dot(prob.astype(BF16), jnp.concatenate([gv[:, c], gav[:, c]], axis=1), ((1,), (0,)))
        gpart[pl.ds(h, 1), :] = jnp.sum(vc[:, c].astype(F32) * both[:, :DIM], axis=0, keepdims=True)
        gval = both[:, DIM:]
        gvo[:, c] = gval[:BLOCK].astype(BF16)
        lastv[:, c] = gval[first:BLOCK]
        gvf[:, c] = gval[BLOCK:]
        return 0

    def backward(h, _):
        c = cols(h)
        prob = st[h]
        dprob = jnp.concatenate([dpt[h], dot(vc[far, c], gav[:, c], ((1,), (1,)))], axis=0)
        row_dot = jnp.sum(prob * dprob, axis=0, keepdims=True)
        ds = (prob * (dprob - row_dot)).astype(BF16)
        gkey = dot(ds, qv[:, c], ((1,), (0,))) * scale
        gqo[:, c] = (dot(ds, kc[:, c], ((0,), (0,))) * scale).astype(BF16)
        gko[:, c] = gkey[:BLOCK].astype(BF16)
        lastk[:, c] = gkey[first:BLOCK]
        for i in range(nb):
            at = slice(BLOCK + i * NY, BLOCK + (i + 1) * NY)
            send[i, :, c] = jnp.concatenate([gkey[at], gvf[pl.ds(i * NY, NY), c]], axis=0).astype(BF16)
        return 0

    def c_copy(c, j, recv):
        p = lax.rem(ib + j, nb)
        s = p if recv else ib
        return pltpu.make_async_remote_copy(
            src_ref=send.at[p, :, chunk(c)], dst_ref=rbuf.at[s, :, chunk(c)],
            send_sem=c_s.at[c, j], recv_sem=c_r.at[c, s],
            device_id=b_peer(p), device_id_type=MESH)

    gain_groups = ((NY, iy, y_peer, gb1), (nb, ib, b_peer, gb2), (ndp, dp, dp_peer, gb3))

    def gain_copy(stage, j, recv):
        size, mine, where, buf = gain_groups[stage]
        p = lax.rem(mine + j, size)
        s = p if recv else mine
        return pltpu.make_async_remote_copy(
            src_ref=buf.at[s], dst_ref=buf.at[s], send_sem=g_s.at[stage, j], recv_sem=g_r.at[stage, s],
            device_id=where(p), device_id_type=MESH)

    def gain_start(stage, value):
        size, mine, _, buf = gain_groups[stage]
        buf[mine] = value
        for j in range(1, size):
            gain_copy(stage, j, False).start()

    def gain_end(stage):
        size, _, _, buf = gain_groups[stage]
        for j in range(1, size):
            gain_copy(stage, j, True).wait_recv()
        total = buf[0]
        for i in range(1, size):
            total = total + buf[i]
        return total

    for c in range(CHUNKS):
        for j in range(1, nb):
            @pl.when(earlier(j))
            def _():
                b_copy(c, j, True).wait_recv()
        for i in range(0, nb, 2):
            one = panel[i, :, chunk(c)].astype(F32)
            two = panel[i + 1, :, chunk(c)].astype(F32)
            at = pl.ds(BLOCK + i * NY, 2 * NY)
            kc[at, chunk(c)] = jnp.concatenate([one[:NY], two[:NY]], axis=0).astype(BF16)
            vc[at, chunk(c)] = jnp.concatenate([one[NY:], two[NY:]], axis=0).astype(BF16)
        lax.fori_loop(c * per, (c + 1) * per, forward, 0, unroll=per)
        if c == CHUNKS - 1:
            gain_start(0, gpart[...])
        lax.fori_loop(c * per, (c + 1) * per, backward, 0, unroll=per)
        for j in range(1, nb):
            @pl.when(earlier(j))
            def _():
                c_copy(c, j, False).start()

    def d_copy(grp, j, recv):
        lo, hi = grp
        p = lax.rem(iy + j, NY)
        cc = pl.ds(lo * width, (hi - lo) * width)
        return pltpu.make_async_remote_copy(
            src_ref=dsend.at[p, :, cc], dst_ref=drecv.at[p if recv else iy, :, cc],
            send_sem=d_s.at[lo, j], recv_sem=d_r.at[lo, p if recv else iy],
            device_id=y_peer(p), device_id_type=MESH)

    def owners(grp):
        lo, hi = grp
        cc = pl.ds(lo * width, (hi - lo) * width)
        acc[:, cc] = send[ib, :, cc].astype(F32)
        for j in range(1, nb):
            @pl.when(later(j))
            def _():
                for c in range(lo, hi):
                    c_copy(c, j, True).wait_recv()
                acc[:, cc] += rbuf[lax.rem(ib + j, nb), :, cc].astype(F32)
        pairs[:, cc] = dot(apart, acc[:, cc].astype(BF16), ((0,), (0,)))
        for i in range(NY):
            dsend[i, :, cc] = pairs[pl.ds(2 * i, 2), cc].astype(BF16)
        for j in range(1, NY):
            d_copy(grp, j, False).start()
        drecv[iy, :, cc] = dsend[iy, :, cc]

    groups = ((0, CHUNKS - 1), (CHUNKS - 1, CHUNKS))
    owners(groups[0])
    gain_start(1, gain_end(0))
    owners(groups[1])
    gain_start(2, gain_end(1))
    for grp in groups:
        for j in range(1, NY):
            d_copy(grp, j, True).wait_recv()
    total = drecv[0].astype(F32)
    for i in range(1, NY):
        total = total + drecv[i].astype(F32)
    last = lax.broadcasted_iota(jnp.int32, (16, features), 0) == 15
    gko[pl.ds(first, 16)] = (lastk[...] + jnp.where(last, total[0:1], 0.0)).astype(BF16)
    gvo[pl.ds(first, 16)] = (lastv[...] + jnp.where(last, total[1:2], 0.0)).astype(BF16)

    gg_ref[...] = gain_end(2) * (1.0 / ndp)

    for j in range(1, NY):
        a_copy(j, False).wait_send()
        for grp in groups:
            d_copy(grp, j, False).wait_send()
    for j in range(1, nb):
        @pl.when(later(j))
        def _():
            for c in range(CHUNKS):
                b_copy(c, j, False).wait_send()

        @pl.when(earlier(j))
        def _():
            for c in range(CHUNKS):
                c_copy(c, j, False).wait_send()
    for stage in range(3):
        for j in range(1, gain_groups[stage][0]):
            gain_copy(stage, j, False).wait_send()


def write_out(a, b, c, d, a_hbm, b_hbm, c_hbm, d_hbm, sem):
    copies = [
        pltpu.make_async_copy(src, dst, sem.at[n])
        for n, (src, dst) in enumerate(((a, a_hbm), (b, b_hbm), (c, c_hbm), (d, d_hbm)))
    ]
    for cp in copies:
        cp.start()
    for cp in copies:
        cp.wait()


def body(ndp, query_proj, key_proj, value_proj, out_grad, out_gain):
    features = query_proj.shape[2]
    heads = features // DIM
    nb = NX * NZ
    blocks = NX * NY * NZ
    flat = lambda a: a.reshape(BLOCK, features)
    hbm = pl.BlockSpec(memory_space=pltpu.HBM)
    vmem = pl.BlockSpec(memory_space=pltpu.VMEM)
    dma = pltpu.SemaphoreType.DMA
    most = max(NY, nb, ndp)
    outs = pl.pallas_call(
        functools.partial(kernel, heads, ndp),
        out_shape=(
            pltpu.VMEM((BLOCK, features), BF16),
            pltpu.VMEM((BLOCK, features), BF16),
            pltpu.VMEM((BLOCK, features), BF16),
            pltpu.VMEM((heads, DIM), F32),
        ),
        in_specs=[hbm] * 5,
        out_specs=(vmem,) * 4,
        scratch_shapes=[
            pltpu.VMEM((BLOCK, features), BF16),
            pltpu.VMEM((BLOCK + blocks, features), BF16),
            pltpu.VMEM((BLOCK + blocks, features), BF16),
            pltpu.VMEM((BLOCK, features), BF16),
            pltpu.VMEM((BLOCK, features), BF16),
            pltpu.VMEM((heads, DIM), F32),
            pltpu.VMEM((16, features), F32),
            pltpu.VMEM((16, features), F32),
            pltpu.VMEM((heads, BLOCK + blocks, BLOCK), F32),
            pltpu.VMEM((heads, BLOCK, BLOCK), F32),
            pltpu.VMEM((blocks, features), F32),
            pltpu.VMEM((NY, 2, features), BF16),
            pltpu.VMEM((nb, 2 * NY, features), BF16),
            pltpu.VMEM((nb, 2 * NY, features), BF16),
            pltpu.VMEM((nb, 2 * NY, features), BF16),
            pltpu.VMEM((2 * NY, features), F32),
            pltpu.VMEM((2 * NY, features), F32),
            pltpu.VMEM((NY, 2, features), BF16),
            pltpu.VMEM((NY, 2, features), BF16),
            pltpu.VMEM((heads, DIM), F32),
            pltpu.VMEM((NY, heads, DIM), F32),
            pltpu.VMEM((nb, heads, DIM), F32),
            pltpu.VMEM((ndp, heads, DIM), F32),
            dma((7,)),
            dma((NY,)),
            dma((NY,)),
            dma((CHUNKS, nb)),
            dma((CHUNKS, nb)),
            dma((CHUNKS, nb)),
            dma((CHUNKS, nb)),
            dma((CHUNKS, NY)),
            dma((CHUNKS, NY)),
            dma((3, most)),
            dma((3, most)),
        ],
        compiler_params=pltpu.CompilerParams(
            collective_id=0, has_side_effects=True, vmem_limit_bytes=52 * 1024 * 1024
        ),
    )(flat(query_proj), flat(key_proj), flat(value_proj), flat(out_grad), out_gain.reshape(heads, DIM))
    rows = jax.ShapeDtypeStruct((BLOCK, features), BF16)
    outs = pl.pallas_call(
        write_out,
        out_shape=(rows, rows, rows, jax.ShapeDtypeStruct((heads, DIM), F32)),
        in_specs=[vmem] * 4,
        out_specs=(hbm,) * 4,
        scratch_shapes=[dma((4,))],
        compiler_params=pltpu.CompilerParams(vmem_limit_bytes=2 * 1024 * 1024),
    )(*outs)
    shape = (1, BLOCK, features)
    return (outs[0].reshape(shape), outs[1].reshape(shape), outs[2].reshape(shape), outs[3].reshape(features))


def solution(mesh):
    spec = P("dp", "ctx", None)
    return jax.shard_map(
        functools.partial(body, mesh.shape["dp"]),
        mesh=mesh,
        in_specs=(spec, spec, spec, spec, P()),
        out_specs=(spec, spec, spec, P()),
        check_vma=False,
    )
```

time: 957 us -> 51.3 us (0.05)
  the two profiles are of different devices: /device:TPU:8 before, /device:TPU:1 now
where the time goes in v2:
time: 51.3 us; the launch traced here: 51.2 us
  Pallas kernels  49.8 us (97%)
  local copies, waits for them, and re-layouts  0.7 us (1%)
  between operations  0.65 us (1%)
    pallas_call x1, Pallas kernels, body(): pl.pallas_call(functools.partial(kernel, heads, ndp), out_shape=(pltpu.VM...  48.5 us
    pallas_call x1, Pallas kernels, body(): pl.pallas_call(write_out, out_shape=(rows, rows, rows, jax.ShapeDtypeStru...  1.31 us

profile of v2, /device:TPU:1, one launch (start us, length us, event | category | flops | bytes accessed | tf_op | source)
XLA Modules:
  0.0 51.2 jit_solution(2958724093564424709)
XLA Ops:
  0.6 0.0 copy-start
  0.6 0.7 %copy-done = f32[2560]{0:T(1024)S(1)} copy-done((f32[2560]{0:T(1024)S(1)}, f32[2560]{0:T(1024)}, u32[]{:S(2)}) %copy-start) | copy-done | bytes 10264
  1.3 48.5 %shard_map.84 = (bf16[128,2560]{1,0:T(8,128)(2,1)S(1)}, bf16[128,2560]{1,0:T(8,128)(2,1)S(1)}, bf16[128,2560]{1,0:T(8,128)(2,1)S(1)}, f32[20,128]{1,0:T(8,128)S(1)}) custom-call(bf16[128,2560]{1,0:T(8,128)(2,1)} %bitcast.10, bf16[128,2560]{1,0:T(8,128)(2,1)} %bitcast.11, bf16[128,2560]{1,0:T(8,128)(2,1)} %bitcast.12, bf16[128,2560]{1,0:T(8,128)(2,1)} %bitcast.13, ...), custom_call_target="tpu_custom_call" | custom-call | tf_op jit(solution)/shard_map/pallas_call | solution.py:335
  49.8 1.3 %shard_map.85 = (bf16[128,2560]{1,0:T(8,128)(2,1)}, bf16[128,2560]{1,0:T(8,128)(2,1)}, bf16[128,2560]{1,0:T(8,128)(2,1)}, f32[20,128]{1,0:T(8,128)}) custom-call(bf16[128,2560]{1,0:T(8,128)(2,1)S(1)} %get-tuple-element.12.a, bf16[128,2560]{1,0:T(8,128)(2,1)S(1)} %get-tuple-element.13.b, bf16[128,2560]{1,0:T(8,128)(2,1)S(1)} %get-tuple-element.14.c, ...), custom_call_target="tpu_custom_call" | custom-call | tf_op jit(solution)/shard_map/pallas_call | solution.py:386
Async XLA Ops:
  0.6 0.7 %copy-start = (f32[2560]{0:T(1024)S(1)}, f32[2560]{0:T(1024)}, u32[]{:S(2)}) copy-start(f32[2560]{0:T(1024)} %param.9) | copy-start | bytes 30724

commit v3 on v2

--- a/solution.py
+++ b/solution.py
@@ -11,10 +11,20 @@
 DIM = 128
 BLOCK = 128
 NX, NY, NZ = 4, 8, 2
-CHUNKS = 4
+CHUNKS = 2
+PAD = 8
 MESH = pl.DeviceIdType.MESH
 F32 = jnp.float32
 BF16 = jnp.bfloat16
+
+
+def y_order():
+    return sorted(range(NY), key=lambda o: (min(o, NY - o), o))
+
+
+def waves():
+    ends = [0, 1, min(5, NY), NY]
+    return [(a, b) for a, b in zip(ends, ends[1:]) if a < b]
 
 
 def dot(a, b, dims):
@@ -26,7 +36,7 @@
     q_hbm, k_hbm, v_hbm, g_hbm, gain_hbm,
     gqo, gko, gvo, gg_ref,
     qv, kc, vc, gv, gav, gain_ref, lastk, lastv, st, dpt,
-    gvf, tails, panel, send, rbuf, acc, pairs, dsend, drecv, gpart, gb1, gb2, gb3,
+    gvf, panel, mixed, send, rbuf, acc, pairs, dsend, drecv, gpart, gb1, gb2, gb3,
     insem, a_s, a_r, b_s, b_r, c_s, c_r, d_s, d_r, g_s, g_r,
 ):
     features = heads * DIM
@@ -42,6 +52,8 @@
     iy = lax.rem(lax.div(me, NZ), NY)
     iz = lax.rem(me, NZ)
     ib = ix * NZ + iz
+    order = y_order()
+    slot_of = [order.index(o) for o in range(NY)]
 
     def y_peer(o):
         return {"ctx": (ix * NY + o) * NZ + iz}
@@ -68,8 +80,6 @@
     load(5, g_hbm, gv)
     load(6, gain_hbm, gain_ref)
 
-    panel[...] = jnp.zeros_like(panel)
-
     barrier = pltpu.get_barrier_semaphore()
 
     def greet(device):
@@ -86,19 +96,58 @@
     loads[1].wait()
     ktail = kc[pl.ds(first, 16)].astype(F32)[15:16]
     vtail = vc[pl.ds(first, 16)].astype(F32)[15:16]
-    tails[iy] = jnp.concatenate([ktail, vtail], axis=0).astype(BF16)
+    panel[ib, 0] = jnp.concatenate([ktail, vtail], axis=0).astype(BF16)
+    gpart[...] = jnp.zeros_like(gpart)
 
     pl.semaphore_wait(barrier, NY + nb + ndp - 3)
 
     def a_copy(j, recv):
         p = lax.rem(iy + j, NY)
-        s = p if recv else iy
+        s = slot_of[j if recv else NY - j]
         return pltpu.make_async_remote_copy(
-            src_ref=tails.at[s], dst_ref=tails.at[s], send_sem=a_s.at[j], recv_sem=a_r.at[s],
+            src_ref=panel.at[ib, 0], dst_ref=panel.at[ib, s], send_sem=a_s.at[j], recv_sem=a_r.at[s],
             device_id=y_peer(p), device_id_type=MESH)
 
-    for j in range(1, NY):
+    def later(j):
+        return lax.div(lax.rem(ib + j, nb), NZ) >= ix
+
+    def earlier(j):
+        return lax.div(lax.rem(ib + j, nb), NZ) <= ix
+
+    pieces = [(0, 1, 0, features)]
+    for c in range(CHUNKS):
+        for lo, hi in waves()[1:]:
+            pieces.append((lo, hi, c * width, width))
+    per_chunk = len(waves()) - 1
+
+    def b_copy(n, j, recv):
+        lo, hi, start, size = pieces[n]
+        p = lax.rem(ib + j, nb)
+        s = p if recv else ib
+        part = (s, pl.ds(lo, hi - lo), slice(None), pl.ds(start, size))
+        return pltpu.make_async_remote_copy(
+            src_ref=panel.at[part], dst_ref=panel.at[part],
+            send_sem=b_s.at[n, j], recv_sem=b_r.at[n, s],
+            device_id=b_peer(p), device_id_type=MESH)
+
+    def send_on(n):
+        for j in range(1, nb):
+            @pl.when(later(j))
+            def _():
+                b_copy(n, j, False).start()
+
+    def wave_here(n):
+        for s in range(max(1, waves()[n][0]), waves()[n][1]):
+            a_copy(order[s], True).wait_recv()
+
+    for j in order[:0:-1]:
         a_copy(j, False).start()
+    send_on(0)
+
+    for j in range(1, nb):
+        @pl.when(jnp.logical_not(earlier(j)))
+        def _():
+            panel[lax.rem(ib + j, nb)] = jnp.zeros(panel.shape[1:], BF16)
 
     key_id = lax.broadcasted_iota(jnp.int32, (BLOCK, BLOCK), 0)
     query_id = lax.broadcasted_iota(jnp.int32, (BLOCK, BLOCK), 1)
@@ -122,68 +171,52 @@
 
     loads[2].wait()
     loads[3].wait()
-    lax.fori_loop(0, heads, local_scores, 0, unroll=per)
+    lax.fori_loop(0, heads, local_scores, 0, unroll=5)
+    wave_here(1)
+    send_on(1)
     loads[4].wait()
     loads[5].wait()
     loads[6].wait()
-    lax.fori_loop(0, heads, local_dprob, 0, unroll=per)
-
-    for j in range(1, NY):
-        a_copy(j, True).wait_recv()
-    for i in range(NY):
-        pairs[pl.ds(2 * i, 2)] = tails[i].astype(F32)
-    to_id = lax.broadcasted_iota(jnp.int32, (2 * NY, 2 * NY), 0)
-    from_id = lax.broadcasted_iota(jnp.int32, (2 * NY, 2 * NY), 1)
-    apart = jnp.where(from_id == 2 * lax.rem(to_id, NY) + lax.div(to_id, NY), 1.0, 0.0).astype(BF16)
-    panel[ib] = dot(apart, pairs[...].astype(BF16), ((1,), (0,))).astype(BF16)
+    lax.fori_loop(0, heads, local_dprob, 0, unroll=5)
+
+    for n in range(2, len(waves())):
+        wave_here(n)
+    for n in range(2, len(pieces)):
+        send_on(n)
+
+    def sorter(n):
+        to_id = lax.broadcasted_iota(jnp.int32, (2 * n, 2 * n), 0)
+        from_id = lax.broadcasted_iota(jnp.int32, (2 * n, 2 * n), 1)
+        return jnp.where(from_id == 2 * lax.rem(to_id, n) + lax.div(to_id, n), 1.0, 0.0).astype(BF16)
 
     def chunk(c):
         return pl.ds(c * width, width)
 
-    def b_copy(c, j, recv):
-        p = lax.rem(ib + j, nb)
-        s = p if recv else ib
-        return pltpu.make_async_remote_copy(
-            src_ref=panel.at[s, :, chunk(c)], dst_ref=panel.at[s, :, chunk(c)],
-            send_sem=b_s.at[c, j], recv_sem=b_r.at[c, s],
-            device_id=b_peer(p), device_id_type=MESH)
-
-    def later(j):
-        return lax.div(lax.rem(ib + j, nb), NZ) >= ix
-
-    def earlier(j):
-        return lax.div(lax.rem(ib + j, nb), NZ) <= ix
-
-    for c in range(CHUNKS):
-        for j in range(1, nb):
-            @pl.when(later(j))
-            def _():
-                b_copy(c, j, False).start()
-
     row = lax.broadcasted_iota(jnp.int32, (blocks, BLOCK), 0)
-    far_id = (lax.div(row, NY * NZ) * NY + lax.rem(row, NY)) * NZ + lax.rem(lax.div(row, NY), NZ)
+    off = jnp.zeros_like(row)
+    for i in range(1, NY):
+        off = jnp.where(lax.rem(row, NY) == i, order[i], off)
+    far_id = (lax.div(row, NY * NZ) * NY + lax.rem(iy + off, NY)) * NZ + lax.rem(lax.div(row, NY), NZ)
     far_keep = far_id < me
     far = pl.ds(BLOCK, blocks)
 
-    def forward(h, _):
+    def fwd(h):
         c = cols(h)
         s_far = jnp.where(far_keep, dot(kc[far, c], qv[:, c], ((1,), (1,))), neg)
         s = jnp.concatenate([st[h, pl.ds(0, BLOCK)], s_far], axis=0)
         top = jnp.max(s, axis=0, keepdims=True)
         e = jnp.exp2((s - top) * escale)
         prob = e * (1.0 / jnp.sum(e, axis=0, keepdims=True))
-        st[h] = prob
         both = dot(prob.astype(BF16), jnp.concatenate([gv[:, c], gav[:, c]], axis=1), ((1,), (0,)))
         gpart[pl.ds(h, 1), :] = jnp.sum(vc[:, c].astype(F32) * both[:, :DIM], axis=0, keepdims=True)
         gval = both[:, DIM:]
         gvo[:, c] = gval[:BLOCK].astype(BF16)
         lastv[:, c] = gval[first:BLOCK]
         gvf[:, c] = gval[BLOCK:]
-        return 0
-
-    def backward(h, _):
+        return prob
+
+    def bwd(h, prob):
         c = cols(h)
-        prob = st[h]
         dprob = jnp.concatenate([dpt[h], dot(vc[far, c], gav[:, c], ((1,), (1,)))], axis=0)
         row_dot = jnp.sum(prob * dprob, axis=0, keepdims=True)
         ds = (prob * (dprob - row_dot)).astype(BF16)
@@ -194,6 +227,17 @@
         for i in range(nb):
             at = slice(BLOCK + i * NY, BLOCK + (i + 1) * NY)
             send[i, :, c] = jnp.concatenate([gkey[at], gvf[pl.ds(i * NY, NY), c]], axis=0).astype(BF16)
+
+    def forward(h, _):
+        st[h] = fwd(h)
+        return 0
+
+    def backward(h, _):
+        bwd(h, st[h])
+        return 0
+
+    def whole(h, _):
+        bwd(h, fwd(h))
         return 0
 
     def c_copy(c, j, recv):
@@ -216,7 +260,8 @@
 
     def gain_start(stage, value):
         size, mine, _, buf = gain_groups[stage]
-        buf[mine] = value
+        for t in range(value.shape[0] // PAD):
+            buf[mine, t] = value[t * PAD : (t + 1) * PAD].astype(BF16)
         for j in range(1, size):
             gain_copy(stage, j, False).start()
 
@@ -224,38 +269,43 @@
         size, _, _, buf = gain_groups[stage]
         for j in range(1, size):
             gain_copy(stage, j, True).wait_recv()
-        total = buf[0]
-        for i in range(1, size):
-            total = total + buf[i]
-        return total
+        total = []
+        for t in range(buf.shape[1]):
+            part = buf[0, t].astype(F32)
+            for i in range(1, size):
+                part = part + buf[i, t].astype(F32)
+            total.append(part)
+        return jnp.concatenate(total, axis=0)
 
     for c in range(CHUNKS):
         for j in range(1, nb):
             @pl.when(earlier(j))
             def _():
-                b_copy(c, j, True).wait_recv()
-        for i in range(0, nb, 2):
-            one = panel[i, :, chunk(c)].astype(F32)
-            two = panel[i + 1, :, chunk(c)].astype(F32)
-            at = pl.ds(BLOCK + i * NY, 2 * NY)
-            kc[at, chunk(c)] = jnp.concatenate([one[:NY], two[:NY]], axis=0).astype(BF16)
-            vc[at, chunk(c)] = jnp.concatenate([one[NY:], two[NY:]], axis=0).astype(BF16)
-        lax.fori_loop(c * per, (c + 1) * per, forward, 0, unroll=per)
-        if c == CHUNKS - 1:
+                for n in [0] * (c == 0) + [1 + c * per_chunk + w for w in range(per_chunk)]:
+                    b_copy(n, j, True).wait_recv()
+        rows = dot(sorter(blocks), panel[:, :, :, chunk(c)].reshape(2 * blocks, width), ((1,), (0,))).astype(BF16)
+        kc[far, chunk(c)] = rows[:blocks]
+        vc[far, chunk(c)] = rows[blocks:]
+        ours = (c * per, (c + 1) * per)
+        if c < CHUNKS - 1:
+            lax.fori_loop(*ours, whole, 0, unroll=per)
+        else:
+            lax.fori_loop(*ours, forward, 0, unroll=per)
             gain_start(0, gpart[...])
-        lax.fori_loop(c * per, (c + 1) * per, backward, 0, unroll=per)
+            lax.fori_loop(*ours, backward, 0, unroll=per)
         for j in range(1, nb):
             @pl.when(earlier(j))
             def _():
                 c_copy(c, j, False).start()
 
-    def d_copy(grp, j, recv):
+    def d_copy(grp, i, recv):
         lo, hi = grp
-        p = lax.rem(iy + j, NY)
+        p = lax.rem(iy + order[i], NY)
+        t = i if recv else slot_of[(NY - order[i]) % NY]
         cc = pl.ds(lo * width, (hi - lo) * width)
         return pltpu.make_async_remote_copy(
-            src_ref=dsend.at[p, :, cc], dst_ref=drecv.at[p if recv else iy, :, cc],
-            send_sem=d_s.at[lo, j], recv_sem=d_r.at[lo, p if recv else iy],
+            src_ref=dsend.at[i, :, cc], dst_ref=drecv.at[t, :, cc],
+            send_sem=d_s.at[lo, i], recv_sem=d_r.at[lo, t],
             device_id=y_peer(p), device_id_type=MESH)
 
     def owners(grp):
@@ -268,17 +318,18 @@
                 for c in range(lo, hi):
                     c_copy(c, j, True).wait_recv()
                 acc[:, cc] += rbuf[lax.rem(ib + j, nb), :, cc].astype(F32)
-        pairs[:, cc] = dot(apart, acc[:, cc].astype(BF16), ((0,), (0,)))
+        pairs[:, cc] = dot(sorter(NY), acc[:, cc].astype(BF16), ((0,), (0,)))
         for i in range(NY):
             dsend[i, :, cc] = pairs[pl.ds(2 * i, 2), cc].astype(BF16)
         for j in range(1, NY):
             d_copy(grp, j, False).start()
-        drecv[iy, :, cc] = dsend[iy, :, cc]
-
-    groups = ((0, CHUNKS - 1), (CHUNKS - 1, CHUNKS))
+        drecv[0, :, cc] = dsend[0, :, cc]
+
+    groups = ((0, CHUNKS - 1), (CHUNKS - 1, CHUNKS)) if CHUNKS > 1 else ((0, 1),)
     owners(groups[0])
     gain_start(1, gain_end(0))
-    owners(groups[1])
+    if len(groups) > 1:
+        owners(groups[1])
     gain_start(2, gain_end(1))
     for grp in groups:
         for j in range(1, NY):
@@ -290,7 +341,7 @@
     gko[pl.ds(first, 16)] = (lastk[...] + jnp.where(last, total[0:1], 0.0)).astype(BF16)
     gvo[pl.ds(first, 16)] = (lastv[...] + jnp.where(last, total[1:2], 0.0)).astype(BF16)
 
-    gg_ref[...] = gain_end(2) * (1.0 / ndp)
+    gg_ref[...] = gain_end(2)[:heads] * (1.0 / ndp)
 
     for j in range(1, NY):
         a_copy(j, False).wait_send()
@@ -299,8 +350,8 @@
     for j in range(1, nb):
         @pl.when(later(j))
         def _():
-            for c in range(CHUNKS):
-                b_copy(c, j, False).wait_send()
+            for n in range(len(pieces)):
+                b_copy(n, j, False).wait_send()
 
         @pl.when(earlier(j))
         def _():
@@ -332,6 +383,8 @@
     vmem = pl.BlockSpec(memory_space=pltpu.VMEM)
     dma = pltpu.SemaphoreType.DMA
     most = max(NY, nb, ndp)
+    tiles = -(-heads // PAD)
+    n_pieces = 1 + (len(waves()) - 1) * CHUNKS
     outs = pl.pallas_call(
         functools.partial(kernel, heads, ndp),
         out_shape=(
@@ -354,23 +407,23 @@
             pltpu.VMEM((heads, BLOCK + blocks, BLOCK), F32),
             pltpu.VMEM((heads, BLOCK, BLOCK), F32),
             pltpu.VMEM((blocks, features), F32),
-            pltpu.VMEM((NY, 2, features), BF16),
-            pltpu.VMEM((nb, 2 * NY, features), BF16),
+            pltpu.VMEM((nb, NY, 2, features), BF16),
+            pltpu.VMEM((2 * blocks, features // CHUNKS), F32),
             pltpu.VMEM((nb, 2 * NY, features), BF16),
             pltpu.VMEM((nb, 2 * NY, features), BF16),
             pltpu.VMEM((2 * NY, features), F32),
             pltpu.VMEM((2 * NY, features), F32),
             pltpu.VMEM((NY, 2, features), BF16),
             pltpu.VMEM((NY, 2, features), BF16),
-            pltpu.VMEM((heads, DIM), F32),
-            pltpu.VMEM((NY, heads, DIM), F32),
-            pltpu.VMEM((nb, heads, DIM), F32),
-            pltpu.VMEM((ndp, heads, DIM), F32),
+            pltpu.VMEM((tiles * PAD, DIM), F32),
+            pltpu.VMEM((NY, tiles, PAD, DIM), BF16),
+            pltpu.VMEM((nb, tiles, PAD, DIM), BF16),
+            pltpu.VMEM((ndp, tiles, PAD, DIM), BF16),
             dma((7,)),
             dma((NY,)),
             dma((NY,)),
-            dma((CHUNKS, nb)),
-            dma((CHUNKS, nb)),
+            dma((n_pieces, nb)),
+            dma((n_pieces, nb)),
             dma((CHUNKS, nb)),
             dma((CHUNKS, nb)),
             dma((CHUNKS, NY)),
@@ -381,7 +434,7 @@
         compiler_params=pltpu.CompilerParams(
             collective_id=0, has_side_effects=True, vmem_limit_bytes=52 * 1024 * 1024
         ),
-    )(flat(query_proj), flat(key_proj), flat(value_proj), flat(out_grad), out_gain.reshape(heads, DIM))
+    )(flat(query_proj), flat(key_proj), flat(value_proj), flat(out_grad), pltpu.with_memory_space_constraint(out_gain.reshape(heads, DIM), pltpu.HBM))
     rows = jax.ShapeDtypeStruct((BLOCK, features), BF16)
     outs = pl.pallas_call(
         write_out,

time: 51.3 us -> 48.2 us (0.940)
  Pallas kernels: 49.8 us -> 47.4 us
  local copies, waits for them, and re-layouts: 0.7 us -> 0 us
    pallas_call x1, Pallas kernels: 48.5 us -> 46.1 us  [body(): pl.pallas_call(functools.partial(kernel, heads, ndp), out_shape=(pltpu.VM...]
    unnamed x2 -> x0, local copies, waits for them, and re-layouts: 0.7 us -> none
where the time goes in v3:
time: 48.2 us; the launch traced here: 48 us
  Pallas kernels  47.4 us (98%)
  between operations  0.64 us (1%)
    pallas_call x1, Pallas kernels, body(): pl.pallas_call(functools.partial(kernel, heads, ndp), out_shape=(pltpu.VM...  46.1 us
    pallas_call x1, Pallas kernels, body(): pl.pallas_call(write_out, out_shape=(rows, rows, rows, jax.ShapeDtypeStru...  1.31 us

profile of v3, /device:TPU:1, one launch (start us, length us, event | category | flops | bytes accessed | tf_op | source)
XLA Modules:
  0.0 48.0 jit_solution(5580522897031321421)
XLA Ops:
  0.6 46.1 %shard_map.84 = (bf16[128,2560]{1,0:T(8,128)(2,1)S(1)}, bf16[128,2560]{1,0:T(8,128)(2,1)S(1)}, bf16[128,2560]{1,0:T(8,128)(2,1)S(1)}, f32[20,128]{1,0:T(8,128)S(1)}) custom-call(bf16[128,2560]{1,0:T(8,128)(2,1)} %bitcast.9, bf16[128,2560]{1,0:T(8,128)(2,1)} %bitcast.10, bf16[128,2560]{1,0:T(8,128)(2,1)} %bitcast.11, bf16[128,2560]{1,0:T(8,128)(2,1)} %bitcast.12, ...), custom_call_target="tpu_custom_call" | custom-call | tf_op jit(solution)/shard_map/pallas_call | solution.py:388
  46.7 1.3 %shard_map.85 = (bf16[128,2560]{1,0:T(8,128)(2,1)}, bf16[128,2560]{1,0:T(8,128)(2,1)}, bf16[128,2560]{1,0:T(8,128)(2,1)}, f32[20,128]{1,0:T(8,128)}) custom-call(bf16[128,2560]{1,0:T(8,128)(2,1)S(1)} %get-tuple-element.12.a, bf16[128,2560]{1,0:T(8,128)(2,1)S(1)} %get-tuple-element.13.b, bf16[128,2560]{1,0:T(8,128)(2,1)S(1)} %get-tuple-element.14.c, ...), custom_call_target="tpu_custom_call" | custom-call | tf_op jit(solution)/shard_map/pallas_call | solution.py:439

commit v4 on v3

--- a/solution.py
+++ b/solution.py
@@ -11,7 +11,6 @@
 DIM = 128
 BLOCK = 128
 NX, NY, NZ = 4, 8, 2
-CHUNKS = 2
 PAD = 8
 MESH = pl.DeviceIdType.MESH
 F32 = jnp.float32
@@ -36,14 +35,14 @@
     q_hbm, k_hbm, v_hbm, g_hbm, gain_hbm,
     gqo, gko, gvo, gg_ref,
     qv, kc, vc, gv, gav, gain_ref, lastk, lastv, st, dpt,
-    gvf, panel, mixed, send, rbuf, acc, pairs, dsend, drecv, gpart, gb1, gb2, gb3,
+    pg, panel, send, rbuf, acc, pairs, dsend, drecv, gpart, gb1, gb2, gb3,
     insem, a_s, a_r, b_s, b_r, c_s, c_r, d_s, d_r, g_s, g_r,
 ):
     features = heads * DIM
     nb = NX * NZ
     blocks = NX * NY * NZ
-    per = heads // CHUNKS
-    width = per * DIM
+    half = heads // 2
+    width = half * DIM
     scale = 1.0 / math.sqrt(DIM)
     escale = scale * math.log2(math.e)
     dp = lax.axis_index("dp")
@@ -64,6 +63,18 @@
     def dp_peer(o):
         return {"dp": o}
 
+    barrier = pltpu.get_barrier_semaphore()
+
+    def greet(device):
+        pl.semaphore_signal(barrier, inc=1, device_id=device, device_id_type=MESH)
+
+    for j in order[:0:-1]:
+        greet(y_peer(lax.rem(iy + j, NY)))
+    for j in range(1, nb):
+        greet(b_peer(lax.rem(ib + j, nb)))
+    for j in range(1, ndp):
+        greet(dp_peer(lax.rem(dp + j, ndp)))
+
     first = BLOCK - 16
     loads = []
 
@@ -80,23 +91,13 @@
     load(5, g_hbm, gv)
     load(6, gain_hbm, gain_ref)
 
-    barrier = pltpu.get_barrier_semaphore()
-
-    def greet(device):
-        pl.semaphore_signal(barrier, inc=1, device_id=device, device_id_type=MESH)
-
-    for j in range(1, NY):
-        greet(y_peer(lax.rem(iy + j, NY)))
-    for j in range(1, nb):
-        greet(b_peer(lax.rem(ib + j, nb)))
-    for j in range(1, ndp):
-        greet(dp_peer(lax.rem(dp + j, ndp)))
-
     loads[0].wait()
     loads[1].wait()
     ktail = kc[pl.ds(first, 16)].astype(F32)[15:16]
     vtail = vc[pl.ds(first, 16)].astype(F32)[15:16]
-    panel[ib, 0] = jnp.concatenate([ktail, vtail], axis=0).astype(BF16)
+    fold = lambda r: jnp.concatenate([r[:, :width], r[:, width:]], axis=0)
+    unfold = lambda r: jnp.concatenate([r[0:1], r[1:2]], axis=1)
+    panel[ib, 0] = jnp.concatenate([fold(ktail), fold(vtail)], axis=1).astype(BF16)
     gpart[...] = jnp.zeros_like(gpart)
 
     pl.semaphore_wait(barrier, NY + nb + ndp - 3)
@@ -115,7 +116,7 @@
         return lax.div(lax.rem(ib + j, nb), NZ) <= ix
 
     pieces = [(0, 1, 0, features)]
-    for c in range(CHUNKS):
+    for c in range(2):
         for lo, hi in waves()[1:]:
             pieces.append((lo, hi, c * width, width))
     per_chunk = len(waves()) - 1
@@ -200,6 +201,23 @@
     far_keep = far_id < me
     far = pl.ds(BLOCK, blocks)
 
+    def take(c):
+        for j in range(1, nb):
+            @pl.when(earlier(j))
+            def _():
+                for n in [0] * (c == 0) + [1 + c * per_chunk + w for w in range(per_chunk)]:
+                    b_copy(n, j, True).wait_recv()
+        rows = dot(sorter(blocks), panel[:, :, :, chunk(c)].reshape(2 * blocks, width), ((1,), (0,))).astype(BF16)
+        buf = (kc, vc)[c]
+        buf[far, pl.ds(0, width)] = rows[:blocks]
+        buf[far, pl.ds(width, width)] = rows[blocks:]
+
+    def keep(start, t, one, two):
+        for i in range(nb):
+            at = slice(i * NY, (i + 1) * NY)
+            send[i, :, pl.ds(pl.multiple_of(start + t * DIM, DIM), DIM)] = (
+                jnp.concatenate([one[at], two[at]], axis=0).astype(BF16))
+
     def fwd(h):
         c = cols(h)
         s_far = jnp.where(far_keep, dot(kc[far, c], qv[:, c], ((1,), (1,))), neg)
@@ -207,16 +225,18 @@
         top = jnp.max(s, axis=0, keepdims=True)
         e = jnp.exp2((s - top) * escale)
         prob = e * (1.0 / jnp.sum(e, axis=0, keepdims=True))
+        st[h] = prob
         both = dot(prob.astype(BF16), jnp.concatenate([gv[:, c], gav[:, c]], axis=1), ((1,), (0,)))
-        gpart[pl.ds(h, 1), :] = jnp.sum(vc[:, c].astype(F32) * both[:, :DIM], axis=0, keepdims=True)
+        gpart[pl.ds(h, 1), :] = jnp.sum(vc[pl.ds(0, BLOCK), c].astype(F32) * both[:BLOCK, :DIM], axis=0, keepdims=True)
+        pg[:, c] = both[BLOCK:, :DIM]
         gval = both[:, DIM:]
         gvo[:, c] = gval[:BLOCK].astype(BF16)
         lastv[:, c] = gval[first:BLOCK]
-        gvf[:, c] = gval[BLOCK:]
-        return prob
-
-    def bwd(h, prob):
+        return gval[BLOCK:]
+
+    def bwd(h):
         c = cols(h)
+        prob = st[h]
         dprob = jnp.concatenate([dpt[h], dot(vc[far, c], gav[:, c], ((1,), (1,)))], axis=0)
         row_dot = jnp.sum(prob * dprob, axis=0, keepdims=True)
         ds = (prob * (dprob - row_dot)).astype(BF16)
@@ -224,27 +244,29 @@
         gqo[:, c] = (dot(ds, kc[:, c], ((0,), (0,))) * scale).astype(BF16)
         gko[:, c] = gkey[:BLOCK].astype(BF16)
         lastk[:, c] = gkey[first:BLOCK]
-        for i in range(nb):
-            at = slice(BLOCK + i * NY, BLOCK + (i + 1) * NY)
-            send[i, :, c] = jnp.concatenate([gkey[at], gvf[pl.ds(i * NY, NY), c]], axis=0).astype(BF16)
-
-    def forward(h, _):
-        st[h] = fwd(h)
+        return gkey[BLOCK:]
+
+    def forward(t, _):
+        keep(width, t, fwd(t), fwd(t + half))
         return 0
 
-    def backward(h, _):
-        bwd(h, st[h])
+    def backward(t, _):
+        keep(0, t, bwd(t), bwd(t + half))
         return 0
 
-    def whole(h, _):
-        bwd(h, fwd(h))
+    def far_gain(h, _):
+        c = cols(h)
+        gpart[pl.ds(h, 1), :] += jnp.sum(vc[far, c].astype(F32) * pg[:, c], axis=0, keepdims=True)
         return 0
 
+    parts = ((width, width), (0, width // 2), (width // 2, width // 2))
+
     def c_copy(c, j, recv):
+        cc = pl.ds(*parts[c])
         p = lax.rem(ib + j, nb)
         s = p if recv else ib
         return pltpu.make_async_remote_copy(
-            src_ref=send.at[p, :, chunk(c)], dst_ref=rbuf.at[s, :, chunk(c)],
+            src_ref=send.at[p, :, cc], dst_ref=rbuf.at[s, :, cc],
             send_sem=c_s.at[c, j], recv_sem=c_r.at[c, s],
             device_id=b_peer(p), device_id_type=MESH)
 
@@ -277,45 +299,40 @@
             total.append(part)
         return jnp.concatenate(total, axis=0)
 
-    for c in range(CHUNKS):
-        for j in range(1, nb):
-            @pl.when(earlier(j))
-            def _():
-                for n in [0] * (c == 0) + [1 + c * per_chunk + w for w in range(per_chunk)]:
-                    b_copy(n, j, True).wait_recv()
-        rows = dot(sorter(blocks), panel[:, :, :, chunk(c)].reshape(2 * blocks, width), ((1,), (0,))).astype(BF16)
-        kc[far, chunk(c)] = rows[:blocks]
-        vc[far, chunk(c)] = rows[blocks:]
-        ours = (c * per, (c + 1) * per)
-        if c < CHUNKS - 1:
-            lax.fori_loop(*ours, whole, 0, unroll=per)
-        else:
-            lax.fori_loop(*ours, forward, 0, unroll=per)
-            gain_start(0, gpart[...])
-            lax.fori_loop(*ours, backward, 0, unroll=per)
+    def send_back(c):
         for j in range(1, nb):
             @pl.when(earlier(j))
             def _():
                 c_copy(c, j, False).start()
 
+    unroll = half // 2
+    take(0)
+    lax.fori_loop(0, half, forward, 0, unroll=unroll)
+    send_back(0)
+    take(1)
+    lax.fori_loop(0, heads, far_gain, 0, unroll=heads)
+    gain_start(0, gpart[...])
+    lax.fori_loop(0, unroll, backward, 0, unroll=unroll)
+    send_back(1)
+    lax.fori_loop(unroll, half, backward, 0, unroll=unroll)
+    send_back(2)
+
     def d_copy(grp, i, recv):
-        lo, hi = grp
         p = lax.rem(iy + order[i], NY)
         t = i if recv else slot_of[(NY - order[i]) % NY]
-        cc = pl.ds(lo * width, (hi - lo) * width)
+        cc = chunk(grp)
         return pltpu.make_async_remote_copy(
             src_ref=dsend.at[i, :, cc], dst_ref=drecv.at[t, :, cc],
-            send_sem=d_s.at[lo, i], recv_sem=d_r.at[lo, t],
+            send_sem=d_s.at[grp, i], recv_sem=d_r.at[grp, t],
             device_id=y_peer(p), device_id_type=MESH)
 
     def owners(grp):
-        lo, hi = grp
-        cc = pl.ds(lo * width, (hi - lo) * width)
+        cc = chunk(grp)
         acc[:, cc] = send[ib, :, cc].astype(F32)
         for j in range(1, nb):
             @pl.when(later(j))
             def _():
-                for c in range(lo, hi):
+                for c in ((1, 2), (0,))[grp]:
                     c_copy(c, j, True).wait_recv()
                 acc[:, cc] += rbuf[lax.rem(ib + j, nb), :, cc].astype(F32)
         pairs[:, cc] = dot(sorter(NY), acc[:, cc].astype(BF16), ((0,), (0,)))
@@ -325,11 +342,10 @@
             d_copy(grp, j, False).start()
         drecv[0, :, cc] = dsend[0, :, cc]
 
-    groups = ((0, CHUNKS - 1), (CHUNKS - 1, CHUNKS)) if CHUNKS > 1 else ((0, 1),)
-    owners(groups[0])
+    groups = (1, 0)
     gain_start(1, gain_end(0))
-    if len(groups) > 1:
-        owners(groups[1])
+    owners(1)
+    owners(0)
     gain_start(2, gain_end(1))
     for grp in groups:
         for j in range(1, NY):
@@ -338,10 +354,8 @@
     for i in range(1, NY):
         total = total + drecv[i].astype(F32)
     last = lax.broadcasted_iota(jnp.int32, (16, features), 0) == 15
-    gko[pl.ds(first, 16)] = (lastk[...] + jnp.where(last, total[0:1], 0.0)).astype(BF16)
-    gvo[pl.ds(first, 16)] = (lastv[...] + jnp.where(last, total[1:2], 0.0)).astype(BF16)
-
-    gg_ref[...] = gain_end(2)[:heads] * (1.0 / ndp)
+    gko[pl.ds(first, 16)] = (lastk[...] + jnp.where(last, unfold(total[:, :width]), 0.0)).astype(BF16)
+    gvo[pl.ds(first, 16)] = (lastv[...] + jnp.where(last, unfold(total[:, width:]), 0.0)).astype(BF16)
 
     for j in range(1, NY):
         a_copy(j, False).wait_send()
@@ -355,11 +369,15 @@
 
         @pl.when(earlier(j))
         def _():
-            for c in range(CHUNKS):
+            for c in range(len(parts)):
                 c_copy(c, j, False).wait_send()
-    for stage in range(3):
+    for stage in range(2):
         for j in range(1, gain_groups[stage][0]):
             gain_copy(stage, j, False).wait_send()
+
+    gg_ref[...] = gain_end(2)[:heads] * (1.0 / ndp)
+    for j in range(1, ndp):
+        gain_copy(2, j, False).wait_send()
 
 
 def write_out(a, b, c, d, a_hbm, b_hbm, c_hbm, d_hbm, sem):
@@ -384,7 +402,7 @@
     dma = pltpu.SemaphoreType.DMA
     most = max(NY, nb, ndp)
     tiles = -(-heads // PAD)
-    n_pieces = 1 + (len(waves()) - 1) * CHUNKS
+    n_pieces = 1 + (len(waves()) - 1) * 2
     outs = pl.pallas_call(
         functools.partial(kernel, heads, ndp),
         out_shape=(
@@ -408,7 +426,6 @@
             pltpu.VMEM((heads, BLOCK, BLOCK), F32),
             pltpu.VMEM((blocks, features), F32),
             pltpu.VMEM((nb, NY, 2, features), BF16),
-            pltpu.VMEM((2 * blocks, features // CHUNKS), F32),
             pltpu.VMEM((nb, 2 * NY, features), BF16),
             pltpu.VMEM((nb, 2 * NY, features), BF16),
             pltpu.VMEM((2 * NY, features), F32),
@@ -424,10 +441,10 @@
             dma((NY,)),
             dma((n_pieces, nb)),
             dma((n_pieces, nb)),
-            dma((CHUNKS, nb)),
-            dma((CHUNKS, nb)),
-            dma((CHUNKS, NY)),
-            dma((CHUNKS, NY)),
+            dma((3, nb)),
+            dma((3, nb)),
+            dma((2, NY)),
+            dma((2, NY)),
             dma((3, most)),
             dma((3, most)),
         ],

time: 48.2 us -> 46.4 us (0.963)
  Pallas kernels: 47.4 us -> 45.6 us
    pallas_call x1, Pallas kernels: 46.1 us -> 44.3 us  [body(): pl.pallas_call(functools.partial(kernel, heads, ndp), out_shape=(pltpu.VM...]
where the time goes in v4:
time: 46.4 us; the launch traced here: 46.3 us
  Pallas kernels  45.6 us (98%)
  between operations  0.64 us (1%)
    pallas_call x1, Pallas kernels, body(): pl.pallas_call(functools.partial(kernel, heads, ndp), out_shape=(pltpu.VM...  44.3 us
    pallas_call x1, Pallas kernels, body(): pl.pallas_call(write_out, out_shape=(rows, rows, rows, jax.ShapeDtypeStru...  1.31 us

profile of v4, /device:TPU:1, one launch (start us, length us, event | category | flops | bytes accessed | tf_op | source)
XLA Modules:
  0.0 46.3 jit_solution(10012755193717665151)
XLA Ops:
  0.6 44.3 %shard_map.84 = (bf16[128,2560]{1,0:T(8,128)(2,1)S(1)}, bf16[128,2560]{1,0:T(8,128)(2,1)S(1)}, bf16[128,2560]{1,0:T(8,128)(2,1)S(1)}, f32[20,128]{1,0:T(8,128)S(1)}) custom-call(bf16[128,2560]{1,0:T(8,128)(2,1)} %bitcast.9, bf16[128,2560]{1,0:T(8,128)(2,1)} %bitcast.10, bf16[128,2560]{1,0:T(8,128)(2,1)} %bitcast.11, bf16[128,2560]{1,0:T(8,128)(2,1)} %bitcast.12, ...), custom_call_target="tpu_custom_call" | custom-call | tf_op jit(solution)/shard_map/pallas_call | solution.py:406
  45.0 1.3 %shard_map.85 = (bf16[128,2560]{1,0:T(8,128)(2,1)}, bf16[128,2560]{1,0:T(8,128)(2,1)}, bf16[128,2560]{1,0:T(8,128)(2,1)}, f32[20,128]{1,0:T(8,128)}) custom-call(bf16[128,2560]{1,0:T(8,128)(2,1)S(1)} %get-tuple-element.12.a, bf16[128,2560]{1,0:T(8,128)(2,1)S(1)} %get-tuple-element.13.b, bf16[128,2560]{1,0:T(8,128)(2,1)S(1)} %get-tuple-element.14.c, ...), custom_call_target="tpu_custom_call" | custom-call | tf_op jit(solution)/shard_map/pallas_call | solution.py:456

commit v5 on v4

--- a/solution.py
+++ b/solution.py
@@ -307,7 +307,7 @@
 
     unroll = half // 2
     take(0)
-    lax.fori_loop(0, half, forward, 0, unroll=unroll)
+    lax.fori_loop(0, half, forward, 0, unroll=half)
     send_back(0)
     take(1)
     lax.fori_loop(0, heads, far_gain, 0, unroll=heads)

time: 46.4 us -> 46.2 us (level)
  no operation moved by 1% of the time
where the time goes in v5:
time: 46.2 us; the launch traced here: 46 us
  Pallas kernels  45.4 us (98%)
  between operations  0.64 us (1%)
    pallas_call x1, Pallas kernels, body(): pl.pallas_call(functools.partial(kernel, heads, ndp), out_shape=(pltpu.VM...  44.1 us
    pallas_call x1, Pallas kernels, body(): pl.pallas_call(write_out, out_shape=(rows, rows, rows, jax.ShapeDtypeStru...  1.31 us

profile of v5, /device:TPU:1, one launch (start us, length us, event | category | flops | bytes accessed | tf_op | source)
XLA Modules:
  0.0 46.0 jit_solution(17626792397946781550)
XLA Ops:
  0.6 44.1 %shard_map.84 = (bf16[128,2560]{1,0:T(8,128)(2,1)S(1)}, bf16[128,2560]{1,0:T(8,128)(2,1)S(1)}, bf16[128,2560]{1,0:T(8,128)(2,1)S(1)}, f32[20,128]{1,0:T(8,128)S(1)}) custom-call(bf16[128,2560]{1,0:T(8,128)(2,1)} %bitcast.9, bf16[128,2560]{1,0:T(8,128)(2,1)} %bitcast.10, bf16[128,2560]{1,0:T(8,128)(2,1)} %bitcast.11, bf16[128,2560]{1,0:T(8,128)(2,1)} %bitcast.12, ...), custom_call_target="tpu_custom_call" | custom-call | tf_op jit(solution)/shard_map/pallas_call | solution.py:406
  44.7 1.3 %shard_map.85 = (bf16[128,2560]{1,0:T(8,128)(2,1)}, bf16[128,2560]{1,0:T(8,128)(2,1)}, bf16[128,2560]{1,0:T(8,128)(2,1)}, f32[20,128]{1,0:T(8,128)}) custom-call(bf16[128,2560]{1,0:T(8,128)(2,1)S(1)} %get-tuple-element.12.a, bf16[128,2560]{1,0:T(8,128)(2,1)S(1)} %get-tuple-element.13.b, bf16[128,2560]{1,0:T(8,128)(2,1)S(1)} %get-tuple-element.14.c, ...), custom_call_target="tpu_custom_call" | custom-call | tf_op jit(solution)/shard_map/pallas_call | solution.py:456
